TPU v7x, 32 devices: a whole 2x2x4 slice. The times are simulated.
32 devices in a mesh: sys: 8 (over z, y), mode: 2 (over x), rank: 2 (over core).
Axes of the slice: x: 2, y: 2, z: 4, core: 2. Of those that a mesh axis runs over, the one named last changes fastest.
Arguments:
- solution_core: bfloat16 [512, 256, 64], P(('sys', 'rank'), 'mode'), parts along dimension 0, may hold values from -6 to 6
- operator_core: bfloat16 [64, 256, 256, 8], P('sys', 'rank', 'mode'), parts along dimension 0, may hold values from -0.125 to 0.125
- left_interface: bfloat16 [512, 8, 64], P('sys', None, 'rank'), parts along dimension 0, may hold values from -0.25 to 0.25
- right_interface: bfloat16 [512, 8, 16], P('sys'), parts along dimension 0, may hold values from -0.75 to 0.75
- rhs_left: bfloat16 [512, 16], P(('sys', 'rank')), parts along dimension 0, may hold values from -1.5 to 1.5
- rhs_core: bfloat16 [128, 256, 16], P('sys', 'mode'), parts along dimension 0, may hold values from -6 to 6
- rhs_right: bfloat16 [128, 16], P('sys'), parts along dimension 0, may hold values from -1.5 to 1.5
Outputs:
- q_core: float32 [512, 256, 80], P(('sys', 'rank'), 'mode'), parts along dimension 0
- r_factor: float32 [640, 80], P('sys'), parts along dimension 0
There are 8 independent parts, one for each index of `sys`. A program takes and returns all parts, laid end to end along the dimension named above; each array names one. Nothing has to cross between parts.
All inputs are finite; a program needn't handle non-finite values.
Results may differ from a plain program's by a relative error of at most 0.0014.
Values may be sent and summed in bfloat16 or wider, within the bound.
A program may use at most 64 MiB of HBM per device.

v0:
```python
import jax
import jax.numpy as jnp
from jax import lax
from jax.sharding import PartitionSpec as P


def per_device(
    solution_core, operator_core, left_interface, right_interface, rhs_left, rhs_core, rhs_right
):
    f32 = jnp.float32
    highest = lax.Precision.HIGHEST
    left_rows, mode_rows, rank_full = solution_core.shape
    resid_rank = right_interface.shape[2]
    core_flat = solution_core.astype(f32).reshape(left_rows * mode_rows, rank_full)
    projected = jnp.einsum(
        "cjd,dyb->cjyb", solution_core, right_interface, preferred_element_type=f32
    ).astype(jnp.bfloat16)
    inter_turned = jnp.transpose(left_interface, (2, 1, 0))
    proj_piece = lax.all_gather(projected, "rank", axis=0, tiled=True)
    inter_piece = lax.all_gather(inter_turned, "rank", axis=0, tiled=True)
    applied = jnp.einsum(
        "xijy,cjyb->cxib", operator_core, proj_piece, preferred_element_type=f32
    ).astype(jnp.bfloat16)
    partial_value = jnp.einsum("cxa,cxib->aib", inter_piece, applied, preferred_element_type=f32)
    turned = lax.all_to_all(partial_value, "rank", split_axis=0, concat_axis=1, tiled=True)
    summed = lax.psum_scatter(turned, "mode", scatter_dimension=1, tiled=True)
    rhs_term = jnp.einsum(
        "af,fig,gb->aib",
        rhs_left.astype(f32),
        rhs_core.astype(f32),
        rhs_right.astype(f32),
        precision=highest,
    )
    residual_core = rhs_term - summed
    resid_flat = residual_core.reshape(left_rows * mode_rows, resid_rank)
    enriched = jnp.concatenate([core_flat, resid_flat], axis=1)
    gram = lax.psum(jnp.dot(enriched.T, enriched, precision=highest), ("mode", "rank"))
    lower = jnp.linalg.cholesky(gram)
    solved = lax.linalg.triangular_solve(
        lower, enriched, left_side=False, lower=True, transpose_a=True
    )
    q_core = solved.reshape(left_rows, mode_rows, rank_full + resid_rank)
    return (q_core, lower.T)


def solution(mesh):
    in_specs = (
        P(("sys", "rank"), "mode", None),
        P("sys", "rank", "mode", None),
        P("sys", None, "rank"),
        P("sys", None, None),
        P(("sys", "rank"), None),
        P("sys", "mode", None),
        P("sys", None),
    )
    out_specs = (P(("sys", "rank"), "mode", None), P("sys", None))
    return jax.shard_map(
        per_device, mesh=mesh, in_specs=in_specs, out_specs=out_specs, check_vma=False
    )
```

profile of v0, /device:TPU:0, one launch (start us, length us, event | category | flops | bytes accessed | tf_op | source)
XLA Modules:
  0.0 88.3 jit_solution(14274479131765673508)
XLA Ops:
  7.2 0.0 copy-start
  7.2 0.0 all-gather.2.cloned.1.call-start
  7.2 2.6 %convolution_convert_fusion = bf16[32,128,8,16]{1,3,2,0:T(8,128)(2,1)} fusion(bf16[32,128,64]{1,2,0:T(8,128)(2,1)} %param.7, bf16[64,8,16]{0,2,1:T(8,128)(2,1)} %param.10), kind=kOutput, calls=%fused_computation.6 | convolution fusion | flops 67633152 | bytes 1589248 | tf_op jit(solution)/shard_map/cjd,dyb->cjyb/dot_general | solution.py:15
  9.8 0.0 all-gather.2.cloned.1.call-update
  9.9 0.0 reduce-scatter.2.cloned.1.call-start
  9.9 2.0 %all_gather.7 = bf16[64,8,64]{2,0,1:T(8,128)(2,1)S(1)} all-gather(bf16[32,8,64]{2,0,1:T(8,128)(2,1)S(1)} %bitcast.87), channel_id=1, replica_groups=mesh['sys'=8,'mode'=2,'rank'=2] {'rank'}, dimensions={0}, use_global_device_ids=true | all-gather | bytes 98304 | tf_op jit(solution)/shard_map/all_gather | solution.py:20
  11.9 11.6 %all-gather.2.cloned.1.call-done = bf16[64,128,8,16]{1,3,2,0:T(8,128)(2,1)} async-done(((bf16[32,128,8,16]{1,3,2,0:T(8,128)(2,1)}), bf16[64,128,8,16]{1,3,2,0:T(8,128)(2,1)}) %all-gather.2.cloned.1.call-update) | async-done | bytes 2097168 | tf_op jit(solution)/shard_map/all_gather | solution.py:19
  23.5 4.6 %fusion.21 = f32[64,128,16]{1,0,2:T(8,128)S(1)} fusion(bf16[8,128,128,8]{2,3,1,0:T(8,128)(2,1)S(1)} %copy-done.5, bf16[64,128,8,16,1]{1,3,2,0,4:T(8,128)(2,1)} %bitcast.88, bf16[64,8,64]{2,0,1:T(8,128)(2,1)S(1)} %all_gather.7), kind=kOutput, calls=%fused_computation.15 | convolution fusion | flops 2282749952 | bytes 4784128 | tf_op jit(solution)/shard_map/cxa,cxib->aib/dot_general | solution.py:24
  28.0 0.3 copy.27
  28.3 0.0 copy-start.1
  28.4 4.3 %all_to_all.18 = f32[64,128,16]{1,2,0:T(8,128)S(1)} all-to-all(f32[64,128,16]{1,2,0:T(8,128)S(1)} %copy.27), channel_id=1, replica_groups=mesh['sys'=8,'mode'=2,'rank'=2] {'rank'}, dimensions={0} | all-to-all | bytes 1048576 | tf_op jit(solution)/shard_map/all_to_all | solution.py:25
  32.6 0.4 copy.72
  33.1 1.2 %all_to_all.16 = f32[32,256,16]{1,0,2:T(8,128)} reshape(f32[32,2,128,16]{2,1,0,3:T(2,128)S(1)} %bitcast.85) | data formatting | bytes 1048576 | tf_op jit(solution)/shard_map/all_to_all | solution.py:25
  34.3 0.0 reduce-scatter.2.cloned.1.call-update
  34.3 0.0 copy-start.4
  34.3 0.1 convert_bitcast_fusion
  34.5 0.1 copy.71
  34.6 0.4 copy-done.4
  35.0 0.2 fusion.37
  35.2 15.0 %reduce-scatter.2.cloned.1.call-done = f32[32,128,16]{1,0,2:T(8,128)} async-done(((f32[32,256,16]{1,0,2:T(8,128)}), f32[32,128,16]{1,0,2:T(8,128)}) %reduce-scatter.2.cloned.1.call-update) | async-done | bytes 262160 | tf_op jit(solution)/shard_map/reduce_scatter | solution.py:26
  50.2 1.2 %fusion.28 = f32[32,128,16]{1,0,2:T(8,128)S(1)} fusion(f32[32,128,16]{1,0,2:T(8,128)} %reduce-scatter.2.cloned.1.call-done, f32[16,16,128]{2,0,1:T(8,128)S(1)} %fusion.37, bf16[32,16]{0,1:T(8,128)(2,1)S(1)} %copy-done.3), kind=kOutput, calls=%fused_computation.17 | convolution fusion | flops 12648448 | bytes 656384 | tf_op jit(solution)/shard_map/af,fig,gb->aib/dot_general | solution.py:27
  51.4 0.2 copy.29
  51.6 0.2 copy.73
  51.8 1.2 %fusion.17 = f32[80,80]{0,1:T(8,128)S(1)} fusion(f32[4096,16]{0,1:T(8,128)S(1)} %bitcast.86, f32[4096,64]{0,1:T(8,128)S(1)} %bitcast.82), kind=kOutput, calls=%fused_computation.11 | convolution fusion | flops 314900480 | bytes 1336320 | tf_op jit(solution)/shard_map/dot_general | solution.py:37
  53.0 10.5 %psum.7 = f32[80,80]{0,1:T(8,128)S(1)} all-reduce(f32[80,80]{0,1:T(8,128)S(1)} %fusion.17), channel_id=1, replica_groups=mesh['sys'=8,'mode'=2,'rank'=2] {'mode','rank'}, use_global_device_ids=true, to_apply=%region_1.0 | all-reduce | flops 6400 | bytes 51200 | tf_op jit(solution)/shard_map/psum | solution.py:37
  63.5 0.1 copy.32
  63.6 7.3 %cholesky.16 = f32[80,80]{1,0:T(8,128)S(1)} custom-call(f32[80,80]{1,0:T(8,128)S(1)} %fusion.33), custom_call_target="Cholesky" | custom-call | tf_op jit(solution)/shard_map/jit(cholesky)/cholesky | solution.py:38
  70.9 0.6 compare_reduce_fusion
  71.6 0.7 fusion.34
  72.2 0.7 copy.34
  73.0 6.1 %custom-call.6 = f32[1,80,80]{1,2,0:T(8,128)S(1)} custom-call(f32[1,80,80]{2,1,0:T(8,128)S(1)} %get-tuple-element.11), custom_call_target="InvertDiagBlocksLowerTriangular" | custom-call | tf_op jit(solution)/shard_map/triangular_solve | solution.py:39
  79.1 2.4 %fusion.13 = f32[32,128,80]{1,2,0:T(8,128)} fusion(f32[32,128,16]{1,2,0:T(8,128)S(1)} %copy.29, f32[32,128,64]{1,2,0:T(8,128)S(1)} %get-tuple-element.9, f32[1,80,80]{1,2,0:T(8,128)S(1)} %custom-call.6), kind=kOutput, calls=%fused_computation.7 | convolution fusion | flops 314900480 | bytes 2647040 | tf_op jit(solution)/shard_map/triangular_solve | solution.py:39
  (10 shorter events, 0.1 us)
Async XLA Ops:
  7.2 27.4 %copy-start = (bf16[16,128,16]{1,2,0:T(8,128)(2,1)S(1)}, bf16[16,128,16]{1,2,0:T(8,128)(2,1)}, u32[]{:S(2)}) copy-start(bf16[16,128,16]{1,2,0:T(8,128)(2,1)} %param.12) | copy-start | bytes 196612
  7.2 2.7 %copy-start.2 = (bf16[64,8,32]{0,2,1:T(8,128)(2,1)S(1)}, bf16[64,8,32]{0,2,1:T(8,128)(2,1)}, u32[]{:S(2)}) copy-start(bf16[64,8,32]{0,2,1:T(8,128)(2,1)} %param.9) | copy-start | bytes 98308
  7.2 16.3 %copy-start.5 = (bf16[8,128,128,8]{2,3,1,0:T(8,128)(2,1)S(1)}, bf16[8,128,128,8]{2,3,1,0:T(8,128)(2,1)}, u32[]{:S(2)}) copy-start(bf16[8,128,128,8]{2,3,1,0:T(8,128)(2,1)} %param.8) | copy-start | bytes 6291460
  7.2 16.3 %all-gather.2.cloned.1.call-start = ((), (), s32[]{:S(2)}) async-start(), calls=%async_computation.2 | async-start | bytes 3145728 | tf_op jit(solution)/shard_map/all_gather | solution.py:19
  9.9 40.3 %reduce-scatter.2.cloned.1.call-start = ((), (), s32[]{:S(2)}) async-start(), calls=%async_computation.3 | async-start | bytes 786432 | tf_op jit(solution)/shard_map/reduce_scatter | solution.py:26
  28.3 5.9 %copy-start.1 = (bf16[32,128,64]{1,2,0:T(8,128)(2,1)S(1)}, bf16[32,128,64]{1,2,0:T(8,128)(2,1)}, u32[]{:S(2)}) copy-start(bf16[32,128,64]{1,2,0:T(8,128)(2,1)} %param.7) | copy-start | bytes 1572868
  34.3 0.7 copy-start.4
  34.3 15.9 %copy-start.3 = (bf16[32,16]{0,1:T(8,128)(2,1)S(1)}, bf16[32,16]{0,1:T(8,128)(2,1)}, u32[]{:S(2)}) copy-start(bf16[32,16]{0,1:T(8,128)(2,1)} %param.11) | copy-start | bytes 3076
Sparse Core Ops, SparseCore 0:
  10.2 13.2 all-gather.1
  34.4 15.7 reduce-scatter.1
where the time goes:
time: 88.6 us; the launch traced here: 88.3 us
  waiting for transfers between devices  26.6 us (30%)
  blocking collectives  16.8 us (19%)
  other arithmetic  14.9 us (17%)
  between operations  14.2 us (16%)
  matrix products  12.1 us (14%)
  local copies, waits for them, and re-layouts  3.55 us (4%)
    reduce_scatter x1, waiting for transfers between devices, per_device(): summed = lax.psum_scatter(turned, 'mode', scatter_dimension=1, tiled=True)  15 us
    all_gather x1, waiting for transfers between devices, per_device(): proj_piece = lax.all_gather(projected, 'rank', axis=0, tiled=True)  11.6 us
    psum x1, blocking collectives, per_device(): lax.psum(jnp.dot(enriched.T, enriched, precision=highest), ('mode', 'rank'))  10.5 us
    another operation x3, other arithmetic, per_device(): lower = jnp.linalg.cholesky(gram)  7.98 us
    another operation x1, other arithmetic, per_device(): lax.linalg.triangular_solve(lower, enriched, left_side=False, lower=True,...  6.13 us
    dot_general x1, matrix products, per_device(): jnp.einsum('cxa,cxib->aib', inter_piece, applied, preferred_element_type=...  4.56 us
    all_to_all x1, blocking collectives, per_device(): lax.all_to_all(partial_value, 'rank', split_axis=0, concat_axis=1, tiled=...  4.29 us
    dot_general x1, matrix products, per_device(): jnp.einsum('cjd,dyb->cjyb', solution_core, right_interface, preferred_ele...  2.58 us
  transfers between devices with their start and end apart: 2, of which 2 were waited for; matrix products, arithmetic and copies ran while one was open for 0% of the time, Pallas kernels for 0%

commit v1 on v0

v1 whole, which is shorter than its diff:
```python
import functools

import jax
import jax.numpy as jnp
from jax import lax
from jax.experimental import pallas as pl
from jax.experimental.pallas import tpu as pltpu
from jax.sharding import PartitionSpec as P

F32 = jnp.float32
BF16 = jnp.bfloat16
MESH = pl.DeviceIdType.MESH
NT = (((1,), (1,)), ((), ()))


def mm(a, b):
    return jnp.dot(a, b, preferred_element_type=F32)


def mm_nt(a, b):
    return lax.dot_general(a, b, NT, preferred_element_type=F32)


def iota(shape, dim):
    return lax.broadcasted_iota(jnp.int32, shape, dim)


def one_hot(cond):
    return jnp.where(cond, 1.0, 0.0).astype(BF16)


def turn(rows, inner, outer):
    row, col = iota((rows, rows), 0), iota((rows, rows), 1)
    return one_hot(col == (row % outer) * inner + row // outer)


def split2(x):
    hi = x.astype(BF16)
    return hi, (x - hi.astype(F32)).astype(BF16)


def term_kernel(
    dims,
    s_hbm, op_hbm, l_hbm, ri_ref, rl_ref, rc_ref, rr_ref,
    res_ref, gram_ref,
    s_all, l_all, op_raw, op2, pblk, z_ref, a_ref, t_ref, tb_ref, t_recv, g_all,
    loc_sem, s_send, s_recv, l_send, l_recv, t_send, t_rsem, g_send, g_recv,
):
    M, R, C, D, J, X, I, Y, A, B, F, G = dims
    m, r = lax.axis_index("mode"), lax.axis_index("rank")
    CT = C * R
    K = D + B

    def others(f):
        for mm_ in range(M):
            for rr_ in range(R):
                pl.when(jnp.logical_not((mm_ == m) & (rr_ == r)))(functools.partial(f, mm_, rr_))

    barrier = pltpu.get_barrier_semaphore()

    def greet(mm_, rr_):
        pl.semaphore_signal(barrier, inc=1, device_id={"mode": mm_, "rank": rr_}, device_id_type=MESH)

    others(greet)
    cp_s = pltpu.make_async_copy(s_hbm, s_all.at[r], loc_sem.at[0])
    cp_l = pltpu.make_async_copy(l_hbm, l_all.at[r], loc_sem.at[1])
    cp_o = pltpu.make_async_copy(op_hbm, op_raw, loc_sem.at[2])
    cp_s.start()
    cp_l.start()
    cp_o.start()
    cp_s.wait()
    cp_l.wait()
    pl.semaphore_wait(barrier, M * R - 1)

    def s_copy(rr_):
        return pltpu.make_async_remote_copy(
            src_ref=s_all.at[r], dst_ref=s_all.at[r], send_sem=s_send.at[rr_], recv_sem=s_recv.at[r],
            device_id={"rank": rr_}, device_id_type=MESH)

    def l_copy(rr_):
        return pltpu.make_async_remote_copy(
            src_ref=l_all.at[r], dst_ref=l_all.at[r], send_sem=l_send.at[rr_], recv_sem=l_recv.at[r],
            device_id={"rank": rr_}, device_id_type=MESH)

    def over_rank(f):
        for rr_ in range(R):
            pl.when(rr_ != r)(functools.partial(f, rr_))

    def start_sl(rr_):
        s_copy(rr_).start()
        l_copy(rr_).start()

    over_rank(start_sl)

    cp_o.wait()
    group = 2 * 128 // Y
    per = 256 // Y
    perm_op = turn(256, Y, per)

    def op_step(g, carry):
        both = jnp.concatenate(
            [op_raw[pl.ds(pl.multiple_of(g * 512, 512), 256), :],
             op_raw[pl.ds(pl.multiple_of(g * 512 + 256, 256), 256), :]], axis=1)
        out = mm(perm_op, both).astype(BF16)
        for h in range(2):
            for y in range(Y):
                op2[pl.ds(pl.multiple_of(g * 2 * per + h * per, per), per), y * J:(y + 1) * J] = (
                    out[y * per:(y + 1) * per, h * J:(h + 1) * J])
        return carry

    lax.fori_loop(0, X * I * Y // 512, op_step, 0, unroll=4)

    AB, FG = C * B, F * G
    row_ab, col_fg = iota((AB, 1), 0), iota((1, FG), 1)
    pick_a = one_hot(row_ab // B == iota((AB, C), 1))
    pick_b = one_hot(row_ab % B == iota((AB, B), 1))
    pick_f = one_hot(iota((F, FG), 0) == col_fg // G)
    pick_g = one_hot(iota((G, FG), 0) == col_fg % G)
    left = mm(mm_nt(pick_a, rl_ref[...]).astype(BF16), pick_f)
    right = mm(mm_nt(pick_b, rr_ref[...]).astype(BF16), pick_g)
    k_hi, k_lo = split2(left * right)
    rc = rc_ref[...]
    res_ref[...] = mm(k_hi, rc) + mm(k_lo, rc)

    ri_t = ri_ref[...]
    perm_cb = turn(16 * B, B, 16)

    def project(rr_):
        for cg in range(C // 16):
            for c2 in range(8):
                c = cg * 16 + c2 * 2
                both = jnp.concatenate(
                    [s_all[rr_, c * D:(c + 1) * D, :], s_all[rr_, (c + 1) * D:(c + 2) * D, :]], axis=1)
                p = mm(ri_t, both).astype(BF16)
                for h in range(2):
                    for y in range(Y):
                        pblk[(c2 * 2 + h) * B:(c2 * 2 + h + 1) * B, y * J:(y + 1) * J] = (
                            p[y * B:(y + 1) * B, h * J:(h + 1) * J])
            zz = mm(perm_cb, pblk[...]).astype(BF16)
            for b in range(B):
                row = pl.multiple_of(b * CT + rr_ * C + cg * 16, 16)
                z_ref[pl.ds(row, 16), :] = zz[b * 16:(b + 1) * 16, :]

    project(r)

    def wait_sl(rr_):
        cp = s_copy(rr_)
        pltpu.make_async_remote_copy(
            src_ref=s_all.at[rr_], dst_ref=s_all.at[rr_], send_sem=s_send.at[rr_], recv_sem=s_recv.at[rr_],
            device_id={"rank": rr_}, device_id_type=MESH).wait_recv()
        pltpu.make_async_remote_copy(
            src_ref=l_all.at[rr_], dst_ref=l_all.at[rr_], send_sem=l_send.at[rr_], recv_sem=l_recv.at[rr_],
            device_id={"rank": rr_}, device_id_type=MESH).wait_recv()
        cp.wait_send()
        l_copy(rr_).wait_send()

    over_rank(wait_sl)
    for k in range(1, R):
        project(lax.rem(r + k, R))

    def main_step(x2, carry):
        w = op2[pl.ds(pl.multiple_of(x2 * 2 * I, 2 * I), 2 * I), :]
        a_ref[x2] = mm_nt(z_ref[...], w).astype(BF16)
        return carry

    lax.fori_loop(0, X // 2, main_step, 0)

    l2 = jnp.concatenate([l_all[rr_] for rr_ in range(R)], axis=0).astype(F32).T.astype(BF16)
    for b2 in range(B // 2):
        cols = []
        for h in range(2):
            b = b2 * 2 + h
            cols.append(jnp.concatenate(
                [a_ref[x // 2, b * CT + rr_ * C:b * CT + (rr_ + 1) * C, (x % 2) * I:(x % 2 + 1) * I]
                 for rr_ in range(R) for x in range(X)], axis=0))
        t = mm(l2, jnp.concatenate(cols, axis=1))
        for h in range(2):
            t_ref[pl.ds(b2 * 2 + h, A, stride=B), :] = t[:, h * I:(h + 1) * I]
    tb_ref[...] = t_ref[...].astype(BF16)

    local = m == r

    def t_copy(rr_):
        return pltpu.make_async_remote_copy(
            src_ref=tb_ref.at[pl.ds(rr_ * AB, AB)], dst_ref=t_recv.at[m],
            send_sem=t_send.at[rr_], recv_sem=t_rsem.at[m],
            device_id={"mode": r, "rank": rr_}, device_id_type=MESH)

    for rr_ in range(R):
        pl.when(jnp.logical_not(local & (rr_ == r)))(lambda rr_=rr_: t_copy(rr_).start())

    @pl.when(local)
    def _():
        res_ref[...] -= t_ref[pl.ds(pl.multiple_of(r * AB, AB), AB), :]

    for mm_ in range(M):
        @pl.when(jnp.logical_not(local & (mm_ == m)))
        def _():
            pltpu.make_async_remote_copy(
                src_ref=tb_ref.at[pl.ds(0, AB)], dst_ref=t_recv.at[mm_],
                send_sem=t_send.at[0], recv_sem=t_rsem.at[mm_],
                device_id={"mode": r, "rank": 0}, device_id_type=MESH).wait_recv()
            res_ref[...] -= t_recv[mm_].astype(F32)

    hi, lo = split2(res_ref[...])
    g = jnp.zeros((D + 2 * B, D + 2 * B), F32)
    for a2 in range(C // 2):
        e = jnp.concatenate(
            [jnp.concatenate([s_all[r, a * D:(a + 1) * D, :], hi[a * B:(a + 1) * B], lo[a * B:(a + 1) * B]], axis=0)
             for a in (2 * a2, 2 * a2 + 1)], axis=1)
        g = g + mm_nt(e, e)
    g = jnp.concatenate([g[:D], g[D:K] + g[K:]], axis=0)
    g = jnp.concatenate([g[:, :D], g[:, D:K] + g[:, K:], jnp.zeros((K, 128 - K), F32)], axis=1)
    me = m * R + r
    g_all[me] = g

    def g_copy(mm_, rr_):
        return pltpu.make_async_remote_copy(
            src_ref=g_all.at[me], dst_ref=g_all.at[me],
            send_sem=g_send.at[mm_ * R + rr_], recv_sem=g_recv.at[me],
            device_id={"mode": mm_, "rank": rr_}, device_id_type=MESH)

    others(lambda mm_, rr_: g_copy(mm_, rr_).start())

    def g_wait(mm_, rr_):
        who = mm_ * R + rr_
        pltpu.make_async_remote_copy(
            src_ref=g_all.at[who], dst_ref=g_all.at[who], send_sem=g_send.at[who], recv_sem=g_recv.at[who],
            device_id={"mode": mm_, "rank": rr_}, device_id_type=MESH).wait_recv()

    others(g_wait)
    total = g_all[0]
    for who in range(1, M * R):
        total = total + g_all[who]
    gram_ref[...] = total
    others(lambda mm_, rr_: g_copy(mm_, rr_).wait_send())
    for rr_ in range(R):
        pl.when(jnp.logical_not(local & (rr_ == r)))(lambda rr_=rr_: t_copy(rr_).wait_send())


def eliminate(rows, n):
    sub = iota((8, 128), 0)
    done = [[None] * 8 for _ in rows]
    rows = [list(x) for x in rows]
    for k in range(n):
        kb, ks = divmod(k, 8)
        ga, ia = rows[kb]
        pivot = ga[ks:ks + 1, k:k + 1]
        inv = lax.rsqrt(pivot)
        grow, irow = ga[ks:ks + 1, :] * inv, ia[ks:ks + 1, :] * inv
        done[kb][ks] = (grow, irow)
        for q in range(kb, len(rows)):
            col = rows[q][0][:, k:k + 1] * inv
            rows[q] = [rows[q][0] - col * grow, rows[q][1] - col * irow]
    return done


def factor_kernel(dims, s_ref, res_ref, gram_ref, q_ref, r_ref):
    M, R, C, D, J, X, I, Y, A, B, F, G = dims
    K = D + B
    eye_row, eye_col = iota((8, 128), 0), iota((8, 128), 1)
    rows = [[gram_ref[8 * q:8 * q + 8, :], jnp.where(eye_col == eye_row + 8 * q, 1.0, 0.0)] for q in range(K // 8)]
    done = eliminate(rows, K)
    upper = jnp.concatenate([x[0] for blk in done for x in blk], axis=0)[:, :K]
    w = jnp.concatenate([x[1] for blk in done for x in blk], axis=0)[:, :K]
    tri = iota((K, K), 1) >= iota((K, K), 0)
    r_ref[...] = jnp.where(tri, upper, 0.0)
    w_hi, w_lo = split2(w)
    lhs = jnp.concatenate([w_hi, w_hi[:, D:], w_lo], axis=1)
    hi, lo = split2(res_ref[...])
    for a2 in range(C // 2):
        cols = []
        for a in (2 * a2, 2 * a2 + 1):
            s, h = s_ref[a * D:(a + 1) * D, :], hi[a * B:(a + 1) * B]
            cols.append(jnp.concatenate([s, h, lo[a * B:(a + 1) * B], s, h], axis=0))
        q = mm(lhs, jnp.concatenate(cols, axis=1))
        q_ref[2 * a2] = q[:, :I]
        q_ref[2 * a2 + 1] = q[:, I:]


def fused(n_mode, n_rank, solution_core, operator_core, left_interface, right_interface, rhs_left, rhs_core, rhs_right):
    C, J, D = solution_core.shape
    X, I, _, Y = operator_core.shape
    A = left_interface.shape[0]
    B = right_interface.shape[2]
    F, _, G = rhs_core.shape
    M, R = n_mode, n_rank
    dims = (M, R, C, D, J, X, I, Y, A, B, F, G)
    K = D + B
    s = solution_core.transpose(0, 2, 1).reshape(C * D, J)
    op = operator_core.transpose(0, 1, 3, 2).reshape(X * I * Y, J)
    li = left_interface.transpose(1, 2, 0).reshape(X * C, A)
    ri = right_interface.transpose(1, 2, 0).reshape(Y * B, D)
    rc = rhs_core.transpose(0, 2, 1).reshape(F * G, I)
    vmem = pl.BlockSpec(memory_space=pltpu.VMEM)
    hbm = pl.BlockSpec(memory_space=pl.ANY)
    DMA = pltpu.SemaphoreType.DMA
    res, gram = pl.pallas_call(
        functools.partial(term_kernel, dims),
        out_shape=(jax.ShapeDtypeStruct((C * B, I), F32), jax.ShapeDtypeStruct((K, 128), F32)),
        in_specs=[hbm, hbm, hbm, vmem, vmem, vmem, vmem],
        out_specs=(vmem, vmem),
        scratch_shapes=[
            pltpu.VMEM((R, C * D, J), BF16),
            pltpu.VMEM((R, X * C, A), BF16),
            pltpu.VMEM((X * I * Y, J), BF16),
            pltpu.VMEM((X * I, Y * J), BF16),
            pltpu.VMEM((16 * B, Y * J), BF16),
            pltpu.VMEM((B * C * R, Y * J), BF16),
            pltpu.VMEM((X // 2, B * C * R, 2 * I), BF16),
            pltpu.VMEM((A * B, I), F32),
            pltpu.VMEM((A * B, I), BF16),
            pltpu.VMEM((M, C * B, I), BF16),
            pltpu.VMEM((M * R, K, 128), F32),
            DMA((3,)), DMA((R,)), DMA((R,)), DMA((R,)), DMA((R,)),
            DMA((R,)), DMA((M,)), DMA((M * R,)), DMA((M * R,)),
        ],
        compiler_params=pltpu.CompilerParams(
            collective_id=0, has_side_effects=True, vmem_limit_bytes=48 * 1024 * 1024),
    )(s, op, li, ri, rhs_left.T, rc, rhs_right)
    q, r_factor = pl.pallas_call(
        functools.partial(factor_kernel, dims),
        out_shape=(jax.ShapeDtypeStruct((C, K, I), F32), jax.ShapeDtypeStruct((K, K), F32)),
        in_specs=[vmem, vmem, vmem],
        out_specs=(vmem, vmem),
        compiler_params=pltpu.CompilerParams(vmem_limit_bytes=48 * 1024 * 1024),
    )(s, res, gram)
    return q.transpose(0, 2, 1), r_factor


def plain(
    n_mode, n_rank, solution_core, operator_core, left_interface, right_interface, rhs_left, rhs_core, rhs_right
):
    highest = lax.Precision.HIGHEST
    left_rows, mode_rows, rank_full = solution_core.shape
    resid_rank = right_interface.shape[2]
    core_flat = solution_core.astype(F32).reshape(left_rows * mode_rows, rank_full)
    projected = jnp.einsum(
        "cjd,dyb->cjyb", solution_core, right_interface, preferred_element_type=F32
    ).astype(BF16)
    inter_turned = jnp.transpose(left_interface, (2, 1, 0))
    proj_piece = lax.all_gather(projected, "rank", axis=0, tiled=True)
    inter_piece = lax.all_gather(inter_turned, "rank", axis=0, tiled=True)
    applied = jnp.einsum(
        "xijy,cjyb->cxib", operator_core, proj_piece, preferred_element_type=F32
    ).astype(BF16)
    partial_value = jnp.einsum("cxa,cxib->aib", inter_piece, applied, preferred_element_type=F32)
    turned = lax.all_to_all(partial_value, "rank", split_axis=0, concat_axis=1, tiled=True)
    summed = lax.psum_scatter(turned, "mode", scatter_dimension=1, tiled=True)
    rhs_term = jnp.einsum(
        "af,fig,gb->aib",
        rhs_left.astype(F32),
        rhs_core.astype(F32),
        rhs_right.astype(F32),
        precision=highest,
    )
    residual_core = rhs_term - summed
    resid_flat = residual_core.reshape(left_rows * mode_rows, resid_rank)
    enriched = jnp.concatenate([core_flat, resid_flat], axis=1)
    gram = lax.psum(jnp.dot(enriched.T, enriched, precision=highest), ("mode", "rank"))
    lower = jnp.linalg.cholesky(gram)
    solved = lax.linalg.triangular_solve(
        lower, enriched, left_side=False, lower=True, transpose_a=True
    )
    q_core = solved.reshape(left_rows, mode_rows, rank_full + resid_rank)
    return (q_core, lower.T)


def per_device(n_mode, n_rank, *args):
    solution_core, operator_core, _, right_interface, _, rhs_core, _ = args
    C, J, D = solution_core.shape
    X, I, _, Y = operator_core.shape
    B = right_interface.shape[2]
    tiles = (
        n_mode == n_rank and J == 128 and I == 128 and rhs_core.shape[1] == I
        and C % 16 == 0 and B == 16 and D % 16 == 0 and D + B <= 128
        and 256 % Y == 0 and (256 // Y) % 16 == 0 and X % 2 == 0
    )
    return (fused if tiles else plain)(n_mode, n_rank, *args)


def solution(mesh):
    in_specs = (
        P(("sys", "rank"), "mode", None),
        P("sys", "rank", "mode", None),
        P("sys", None, "rank"),
        P("sys", None, None),
        P(("sys", "rank"), None),
        P("sys", "mode", None),
        P("sys", None),
    )
    out_specs = (P(("sys", "rank"), "mode", None), P("sys", None))
    return jax.shard_map(
        functools.partial(per_device, mesh.shape["mode"], mesh.shape["rank"]),
        mesh=mesh, in_specs=in_specs, out_specs=out_specs, check_vma=False,
    )
```

time: 88.6 us -> 34.2 us (0.39)
  Pallas kernels: 0 us -> 26.7 us
  waiting for transfers between devices: 26.6 us -> 0 us
  blocking collectives: 16.8 us -> 0 us
  other arithmetic: 14.9 us -> 0 us
  between operations: 14.2 us -> 0.65 us
  matrix products: 12.1 us -> 0 us
  local copies, waits for them, and re-layouts: 3.55 us -> 6.43 us
    pallas_call x0 -> x2, Pallas kernels: none -> 26.7 us  [the longest x1 18.7 us: fused(): pl.pallas_call(functools.partial(term_kernel, dims), out_shape=(jax.Shape...]
    reduce_scatter x1 -> x0, waiting for transfers between devices: 15 us -> none  [per_device(): summed = lax.psum_scatter(turned, 'mode', scatter_dimension=1, tiled=True)]
    another operation x4 -> x0, other arithmetic: 14.1 us -> none  [the longest x3 7.98 us: per_device(): lower = jnp.linalg.cholesky(gram)]
    all_gather x1 -> x0, waiting for transfers between devices: 11.6 us -> none  [per_device(): proj_piece = lax.all_gather(projected, 'rank', axis=0, tiled=True)]
    psum x1 -> x0, blocking collectives: 10.5 us -> none  [per_device(): lax.psum(jnp.dot(enriched.T, enriched, precision=highest), ('mode', 'rank'))]
    dot_general x5 -> x0, matrix products: 9.75 us -> none  [the longest x1 4.56 us: per_device(): jnp.einsum('cxa,cxib->aib', inter_piece, applied, preferred_element_type=...]
    unnamed x14, local copies, waits for them, and re-layouts: 1.32 us -> 6.43 us
    all_to_all x1 -> x0, blocking collectives: 4.29 us -> none  [per_device(): lax.all_to_all(partial_value, 'rank', split_axis=0, concat_axis=1, tiled=...]
  transfers between devices with their start and end apart: 2 -> 0, of which waited for: 2 -> 0; matrix products, arithmetic and copies ran while one was open for 0% -> 0% of each run, Pallas kernels for 0% -> 0%
where the time goes in v1:
time: 34.2 us; the launch traced here: 33.8 us
  Pallas kernels  26.7 us (78%)
  local copies, waits for them, and re-layouts  6.43 us (19%)
  between operations  0.65 us (2%)
    pallas_call x1, Pallas kernels, fused(): pl.pallas_call(functools.partial(term_kernel, dims), out_shape=(jax.Shape...  18.7 us
    pallas_call x1, Pallas kernels, fused(): pl.pallas_call(functools.partial(factor_kernel, dims), out_shape=(jax.Sha...  8.01 us
    unnamed x14, local copies, waits for them, and re-layouts  6.43 us

profile of v1, /device:TPU:0, one launch (start us, length us, event | category | flops | bytes accessed | tf_op | source)
XLA Modules:
  0.0 33.8 jit_solution(6158329652492923000)
XLA Ops:
  0.6 0.0 copy-start
  0.6 1.6 %copy-done = bf16[8,128,128,8]{2,3,1,0:T(8,128)(2,1)S(1)} copy-done((bf16[8,128,128,8]{2,3,1,0:T(8,128)(2,1)S(1)}, bf16[8,128,128,8]{2,3,1,0:T(8,128)(2,1)}, u32[]{:S(2)}) %copy-start) | copy-done | bytes 2097176
  2.2 0.0 copy-start.1
  2.2 1.0 %copy-done.1 = bf16[32,128,64]{1,2,0:T(8,128)(2,1)S(1)} copy-done((bf16[32,128,64]{1,2,0:T(8,128)(2,1)S(1)}, bf16[32,128,64]{1,2,0:T(8,128)(2,1)}, u32[]{:S(2)}) %copy-start.1) | copy-done | bytes 524312
  3.3 0.0 copy-start.2
  3.3 0.8 %copy-done.2 = bf16[64,8,32]{0,2,1:T(8,128)(2,1)S(1)} copy-done((bf16[64,8,32]{0,2,1:T(8,128)(2,1)S(1)}, bf16[64,8,32]{0,2,1:T(8,128)(2,1)}, u32[]{:S(2)}) %copy-start.2) | copy-done | bytes 32792
  4.1 0.0 copy-start.3
  4.1 0.8 %copy-done.3 = bf16[16,128,16]{1,2,0:T(8,128)(2,1)S(1)} copy-done((bf16[16,128,16]{1,2,0:T(8,128)(2,1)S(1)}, bf16[16,128,16]{1,2,0:T(8,128)(2,1)}, u32[]{:S(2)}) %copy-start.3) | copy-done | bytes 65560
  4.9 0.0 copy-start.4
  4.9 0.8 %copy-done.4 = bf16[64,8,16]{0,2,1:T(8,128)(2,1)S(1)} copy-done((bf16[64,8,16]{0,2,1:T(8,128)(2,1)S(1)}, bf16[64,8,16]{0,2,1:T(8,128)(2,1)}, u32[]{:S(2)}) %copy-start.4) | copy-done | bytes 16408
  5.7 0.0 copy-start.5
  5.7 0.7 %copy-done.5 = bf16[32,16]{0,1:T(8,128)(2,1)S(1)} copy-done((bf16[32,16]{0,1:T(8,128)(2,1)S(1)}, bf16[32,16]{0,1:T(8,128)(2,1)}, u32[]{:S(2)}) %copy-start.5) | copy-done | bytes 1048
  6.4 0.0 copy-start.6
  6.4 0.7 %copy-done.6 = bf16[16,16]{1,0:T(8,128)(2,1)S(1)} copy-done((bf16[16,16]{1,0:T(8,128)(2,1)S(1)}, bf16[16,16]{1,0:T(8,128)(2,1)}, u32[]{:S(2)}) %copy-start.6) | copy-done | bytes 536
  7.1 18.7 %shard_map.86 = (f32[512,128]{1,0:T(8,128)S(1)}, f32[80,128]{1,0:T(8,128)S(1)}) custom-call(bf16[2048,128]{1,0:T(8,128)(2,1)S(1)} %bitcast.18, bf16[8192,128]{1,0:T(8,128)(2,1)S(1)} %bitcast.17, bf16[256,64]{1,0:T(8,128)(2,1)S(1)} %bitcast.20, bf16[128,64]{1,0:T(8,128)(2,1)S(1)} %bitcast.22, bf16[16,32]{1,0:T(8,128)(2,1)S(1)} %bitcast.23, ...), custom_call_target="tpu_custom_call" | custom-call | tf_op jit(solution)/shard_map/pallas_call | solution.py:298
  25.8 8.0 %shard_map.87 = (f32[32,80,128]{2,1,0:T(8,128)}, f32[80,80]{1,0:T(8,128)}) custom-call(bf16[2048,128]{1,0:T(8,128)(2,1)S(1)} %bitcast.19, f32[512,128]{1,0:T(8,128)S(1)} %get-tuple-element.6.res_ref, f32[80,128]{1,0:T(8,128)S(1)} %get-tuple-element.7.gram_ref), custom_call_target="tpu_custom_call" | custom-call | tf_op jit(solution)/shard_map/pallas_call | solution.py:321
Async XLA Ops:
  0.6 1.6 %copy-start = (bf16[8,128,128,8]{2,3,1,0:T(8,128)(2,1)S(1)}, bf16[8,128,128,8]{2,3,1,0:T(8,128)(2,1)}, u32[]{:S(2)}) copy-start(bf16[8,128,128,8]{2,3,1,0:T(8,128)(2,1)} %param.8) | copy-start | bytes 6291460
  2.2 1.0 %copy-start.1 = (bf16[32,128,64]{1,2,0:T(8,128)(2,1)S(1)}, bf16[32,128,64]{1,2,0:T(8,128)(2,1)}, u32[]{:S(2)}) copy-start(bf16[32,128,64]{1,2,0:T(8,128)(2,1)} %param.7) | copy-start | bytes 1572868
  3.3 0.8 %copy-start.2 = (bf16[64,8,32]{0,2,1:T(8,128)(2,1)S(1)}, bf16[64,8,32]{0,2,1:T(8,128)(2,1)}, u32[]{:S(2)}) copy-start(bf16[64,8,32]{0,2,1:T(8,128)(2,1)} %param.9) | copy-start | bytes 98308
  4.1 0.8 %copy-start.3 = (bf16[16,128,16]{1,2,0:T(8,128)(2,1)S(1)}, bf16[16,128,16]{1,2,0:T(8,128)(2,1)}, u32[]{:S(2)}) copy-start(bf16[16,128,16]{1,2,0:T(8,128)(2,1)} %param.12) | copy-start | bytes 196612
  4.9 0.8 %copy-start.4 = (bf16[64,8,16]{0,2,1:T(8,128)(2,1)S(1)}, bf16[64,8,16]{0,2,1:T(8,128)(2,1)}, u32[]{:S(2)}) copy-start(bf16[64,8,16]{0,2,1:T(8,128)(2,1)} %param.10) | copy-start | bytes 49156
  5.7 0.7 %copy-start.5 = (bf16[32,16]{0,1:T(8,128)(2,1)S(1)}, bf16[32,16]{0,1:T(8,128)(2,1)}, u32[]{:S(2)}) copy-start(bf16[32,16]{0,1:T(8,128)(2,1)} %param.11) | copy-start | bytes 3076
  6.4 0.7 %copy-start.6 = (bf16[16,16]{1,0:T(8,128)(2,1)S(1)}, bf16[16,16]{1,0:T(8,128)(2,1)}, u32[]{:S(2)}) copy-start(bf16[16,16]{1,0:T(8,128)(2,1)} %rr_ref.1) | copy-start | bytes 1540

commit v2 on v1

--- a/solution.py
+++ b/solution.py
@@ -41,9 +41,9 @@
 
 def term_kernel(
     dims,
-    s_hbm, op_hbm, l_hbm, ri_ref, rl_ref, rc_ref, rr_ref,
+    s_hbm, op_hbm, l_hbm, ri_hbm, rl_hbm, rc_hbm, rr_hbm,
     res_ref, gram_ref,
-    s_all, l_all, op_raw, op2, pblk, z_ref, a_ref, t_ref, tb_ref, t_recv, g_all,
+    ri_ref, rl_ref, rc_ref, rr_ref, s_all, l_all, op_raw, op2, pblk, z_ref, a_ref, t_ref, tb_ref, t_recv, g_all,
     loc_sem, s_send, s_recv, l_send, l_recv, t_send, t_rsem, g_send, g_recv,
 ):
     M, R, C, D, J, X, I, Y, A, B, F, G = dims
@@ -65,9 +65,16 @@
     cp_s = pltpu.make_async_copy(s_hbm, s_all.at[r], loc_sem.at[0])
     cp_l = pltpu.make_async_copy(l_hbm, l_all.at[r], loc_sem.at[1])
     cp_o = pltpu.make_async_copy(op_hbm, op_raw, loc_sem.at[2])
+    small = [
+        pltpu.make_async_copy(src, dst, loc_sem.at[3 + k])
+        for k, (src, dst) in enumerate(
+            ((ri_hbm, ri_ref), (rl_hbm, rl_ref), (rc_hbm, rc_ref), (rr_hbm, rr_ref)))
+    ]
     cp_s.start()
     cp_l.start()
     cp_o.start()
+    for cp in small:
+        cp.start()
     cp_s.wait()
     cp_l.wait()
     pl.semaphore_wait(barrier, M * R - 1)
@@ -109,6 +116,9 @@
         return carry
 
     lax.fori_loop(0, X * I * Y // 512, op_step, 0, unroll=4)
+
+    for cp in small:
+        cp.wait()
 
     AB, FG = C * B, F * G
     row_ab, col_fg = iota((AB, 1), 0), iota((1, FG), 1)
@@ -255,9 +265,11 @@
     return done
 
 
-def factor_kernel(dims, s_ref, res_ref, gram_ref, q_ref, r_ref):
+def factor_kernel(dims, s_hbm, res_ref, gram_ref, q_ref, r_ref, s_ref, sem):
     M, R, C, D, J, X, I, Y, A, B, F, G = dims
     K = D + B
+    cp = pltpu.make_async_copy(s_hbm, s_ref, sem)
+    cp.start()
     eye_row, eye_col = iota((8, 128), 0), iota((8, 128), 1)
     rows = [[gram_ref[8 * q:8 * q + 8, :], jnp.where(eye_col == eye_row + 8 * q, 1.0, 0.0)] for q in range(K // 8)]
     done = eliminate(rows, K)
@@ -268,6 +280,7 @@
     w_hi, w_lo = split2(w)
     lhs = jnp.concatenate([w_hi, w_hi[:, D:], w_lo], axis=1)
     hi, lo = split2(res_ref[...])
+    cp.wait()
     for a2 in range(C // 2):
         cols = []
         for a in (2 * a2, 2 * a2 + 1):
@@ -292,15 +305,20 @@
     li = left_interface.transpose(1, 2, 0).reshape(X * C, A)
     ri = right_interface.transpose(1, 2, 0).reshape(Y * B, D)
     rc = rhs_core.transpose(0, 2, 1).reshape(F * G, I)
+    rl = rhs_left.T
     vmem = pl.BlockSpec(memory_space=pltpu.VMEM)
     hbm = pl.BlockSpec(memory_space=pl.ANY)
     DMA = pltpu.SemaphoreType.DMA
     res, gram = pl.pallas_call(
         functools.partial(term_kernel, dims),
         out_shape=(jax.ShapeDtypeStruct((C * B, I), F32), jax.ShapeDtypeStruct((K, 128), F32)),
-        in_specs=[hbm, hbm, hbm, vmem, vmem, vmem, vmem],
+        in_specs=[hbm] * 7,
         out_specs=(vmem, vmem),
         scratch_shapes=[
+            pltpu.VMEM(ri.shape, BF16),
+            pltpu.VMEM(rl.shape, BF16),
+            pltpu.VMEM(rc.shape, BF16),
+            pltpu.VMEM(rhs_right.shape, BF16),
             pltpu.VMEM((R, C * D, J), BF16),
             pltpu.VMEM((R, X * C, A), BF16),
             pltpu.VMEM((X * I * Y, J), BF16),
@@ -312,18 +330,19 @@
             pltpu.VMEM((A * B, I), BF16),
             pltpu.VMEM((M, C * B, I), BF16),
             pltpu.VMEM((M * R, K, 128), F32),
-            DMA((3,)), DMA((R,)), DMA((R,)), DMA((R,)), DMA((R,)),
+            DMA((7,)), DMA((R,)), DMA((R,)), DMA((R,)), DMA((R,)),
             DMA((R,)), DMA((M,)), DMA((M * R,)), DMA((M * R,)),
         ],
         compiler_params=pltpu.CompilerParams(
-            collective_id=0, has_side_effects=True, vmem_limit_bytes=48 * 1024 * 1024),
-    )(s, op, li, ri, rhs_left.T, rc, rhs_right)
+            collective_id=0, has_side_effects=True, vmem_limit_bytes=62 * 1024 * 1024),
+    )(s, op, li, ri, rl, rc, rhs_right)
     q, r_factor = pl.pallas_call(
         functools.partial(factor_kernel, dims),
         out_shape=(jax.ShapeDtypeStruct((C, K, I), F32), jax.ShapeDtypeStruct((K, K), F32)),
-        in_specs=[vmem, vmem, vmem],
+        in_specs=[hbm, vmem, vmem],
         out_specs=(vmem, vmem),
-        compiler_params=pltpu.CompilerParams(vmem_limit_bytes=48 * 1024 * 1024),
+        scratch_shapes=[pltpu.VMEM(s.shape, BF16), DMA],
+        compiler_params=pltpu.CompilerParams(vmem_limit_bytes=62 * 1024 * 1024),
     )(s, res, gram)
     return q.transpose(0, 2, 1), r_factor
 

time: 34.2 us -> 29.3 us (0.86)
  local copies, waits for them, and re-layouts: 6.43 us -> 0 us
  Pallas kernels: 26.7 us -> 28.5 us
    unnamed x14 -> x0, local copies, waits for them, and re-layouts: 6.43 us -> none
    pallas_call x1, Pallas kernels: 8.01 us -> 9.05 us  [fused(): pl.pallas_call(functools.partial(factor_kernel, dims), out_shape=(jax.Sha...]
    pallas_call x1, Pallas kernels: 18.7 us -> 19.5 us  [fused(): pl.pallas_call(functools.partial(term_kernel, dims), out_shape=(jax.Shape...]
where the time goes in v2:
time: 29.3 us; the launch traced here: 29.2 us
  Pallas kernels  28.5 us (97%)
  between operations  0.64 us (2%)
    pallas_call x1, Pallas kernels, fused(): pl.pallas_call(functools.partial(term_kernel, dims), out_shape=(jax.Shape...  19.5 us
    pallas_call x1, Pallas kernels, fused(): pl.pallas_call(functools.partial(factor_kernel, dims), out_shape=(jax.Sha...  9.05 us

profile of v2, /device:TPU:0, one launch (start us, length us, event | category | flops | bytes accessed | tf_op | source)
XLA Modules:
  0.0 29.2 jit_solution(3966490308290684077)
XLA Ops:
  0.6 19.5 %shard_map.86 = (f32[512,128]{1,0:T(8,128)}, f32[80,128]{1,0:T(8,128)}) custom-call(bf16[2048,128]{1,0:T(8,128)(2,1)} %bitcast.18, bf16[8192,128]{1,0:T(8,128)(2,1)} %bitcast.17, bf16[256,64]{1,0:T(8,128)(2,1)} %bitcast.20, bf16[128,64]{1,0:T(8,128)(2,1)} %bitcast.22, bf16[16,32]{1,0:T(8,128)(2,1)} %bitcast.23, bf16[256,128]{1,0:T(8,128)(2,1)} %bitcast.21, ...), custom_call_target="tpu_custom_call" | custom-call | tf_op jit(solution)/shard_map/pallas_call | solution.py:312
  20.1 9.1 %shard_map.87 = (f32[32,80,128]{2,1,0:T(8,128)}, f32[80,80]{1,0:T(8,128)}) custom-call(bf16[2048,128]{1,0:T(8,128)(2,1)} %bitcast.19, f32[512,128]{1,0:T(8,128)} %get-tuple-element.6.res_ref, f32[80,128]{1,0:T(8,128)} %get-tuple-element.7.gram_ref), custom_call_target="tpu_custom_call" | custom-call | tf_op jit(solution)/shard_map/pallas_call | solution.py:339

commit v3 on v2

--- a/solution.py
+++ b/solution.py
@@ -42,9 +42,9 @@
 def term_kernel(
     dims,
     s_hbm, op_hbm, l_hbm, ri_hbm, rl_hbm, rc_hbm, rr_hbm,
-    res_ref, gram_ref,
-    ri_ref, rl_ref, rc_ref, rr_ref, s_all, l_all, op_raw, op2, pblk, z_ref, a_ref, t_ref, tb_ref, t_recv, g_all,
-    loc_sem, s_send, s_recv, l_send, l_recv, t_send, t_rsem, g_send, g_recv,
+    res_ref, gram_ref, fac_ref,
+    ri_ref, rl_ref, rc_ref, rr_ref, s_all, l_all, op_raw, op2, pblk, z_ref, a_ref, t_ref, tb_ref, t_recv, g_all, gs_all,
+    loc_sem, s_send, s_recv, l_send, l_recv, t_send, t_rsem, g_send, g_recv, gs_send, gs_recv,
 ):
     M, R, C, D, J, X, I, Y, A, B, F, G = dims
     m, r = lax.axis_index("mode"), lax.axis_index("rank")
@@ -99,6 +99,39 @@
 
     over_rank(start_sl)
 
+    me = m * R + r
+    gs = jnp.zeros((D, D), F32)
+    for a2 in range(C // 2):
+        e = jnp.concatenate([s_all[r, a * D:(a + 1) * D, :] for a in (2 * a2, 2 * a2 + 1)], axis=1)
+        gs = gs + mm_nt(e, e)
+    gs_all[me] = jnp.concatenate([gs, jnp.zeros((D, 128 - D), F32)], axis=1)
+
+    def sums(buf, send, recv):
+        def copy(who, mm_, rr_):
+            return pltpu.make_async_remote_copy(
+                src_ref=buf.at[who], dst_ref=buf.at[who],
+                send_sem=send.at[mm_ * R + rr_], recv_sem=recv.at[who],
+                device_id={"mode": mm_, "rank": rr_}, device_id_type=MESH)
+
+        def start():
+            others(lambda mm_, rr_: copy(me, mm_, rr_).start())
+
+        def finish():
+            others(lambda mm_, rr_: copy(mm_ * R + rr_, mm_, rr_).wait_recv())
+            total = buf[0]
+            for who in range(1, M * R):
+                total = total + buf[who]
+            return total
+
+        def sent():
+            others(lambda mm_, rr_: copy(me, mm_, rr_).wait_send())
+
+        return start, finish, sent
+
+    gs_start, gs_finish, gs_sent = sums(gs_all, gs_send, gs_recv)
+    g_start, g_finish, g_sent = sums(g_all, g_send, g_recv)
+    gs_start()
+
     cp_o.wait()
     group = 2 * 128 // Y
     per = 256 // Y
@@ -199,6 +232,8 @@
     for rr_ in range(R):
         pl.when(jnp.logical_not(local & (rr_ == r)))(lambda rr_=rr_: t_copy(rr_).start())
 
+    fac_ref[...] = eliminate(gs_finish(), D)
+
     @pl.when(local)
     def _():
         res_ref[...] -= t_ref[pl.ds(pl.multiple_of(r * AB, AB), AB), :]
@@ -213,68 +248,56 @@
             res_ref[...] -= t_recv[mm_].astype(F32)
 
     hi, lo = split2(res_ref[...])
-    g = jnp.zeros((D + 2 * B, D + 2 * B), F32)
+    g = jnp.zeros((2 * B, D + 2 * B), F32)
     for a2 in range(C // 2):
-        e = jnp.concatenate(
-            [jnp.concatenate([s_all[r, a * D:(a + 1) * D, :], hi[a * B:(a + 1) * B], lo[a * B:(a + 1) * B]], axis=0)
+        hl = jnp.concatenate(
+            [jnp.concatenate([hi[a * B:(a + 1) * B], lo[a * B:(a + 1) * B]], axis=0)
              for a in (2 * a2, 2 * a2 + 1)], axis=1)
-        g = g + mm_nt(e, e)
-    g = jnp.concatenate([g[:D], g[D:K] + g[K:]], axis=0)
-    g = jnp.concatenate([g[:, :D], g[:, D:K] + g[:, K:], jnp.zeros((K, 128 - K), F32)], axis=1)
-    me = m * R + r
-    g_all[me] = g
-
-    def g_copy(mm_, rr_):
-        return pltpu.make_async_remote_copy(
-            src_ref=g_all.at[me], dst_ref=g_all.at[me],
-            send_sem=g_send.at[mm_ * R + rr_], recv_sem=g_recv.at[me],
-            device_id={"mode": mm_, "rank": rr_}, device_id_type=MESH)
-
-    others(lambda mm_, rr_: g_copy(mm_, rr_).start())
-
-    def g_wait(mm_, rr_):
-        who = mm_ * R + rr_
-        pltpu.make_async_remote_copy(
-            src_ref=g_all.at[who], dst_ref=g_all.at[who], send_sem=g_send.at[who], recv_sem=g_recv.at[who],
-            device_id={"mode": mm_, "rank": rr_}, device_id_type=MESH).wait_recv()
-
-    others(g_wait)
-    total = g_all[0]
-    for who in range(1, M * R):
-        total = total + g_all[who]
-    gram_ref[...] = total
-    others(lambda mm_, rr_: g_copy(mm_, rr_).wait_send())
+        e = jnp.concatenate([s_all[r, a * D:(a + 1) * D, :] for a in (2 * a2, 2 * a2 + 1)], axis=1)
+        g = g + mm_nt(hl, jnp.concatenate([e, hl], axis=0))
+    g = g[:B] + g[B:]
+    g_all[me] = jnp.concatenate([g[:, :D], g[:, D:K] + g[:, K:], jnp.zeros((B, 128 - K), F32)], axis=1)
+    g_start()
+    gram_ref[...] = g_finish()
+    g_sent()
+    gs_sent()
     for rr_ in range(R):
         pl.when(jnp.logical_not(local & (rr_ == r)))(lambda rr_=rr_: t_copy(rr_).wait_send())
 
 
-def eliminate(rows, n):
-    sub = iota((8, 128), 0)
-    done = [[None] * 8 for _ in rows]
-    rows = [list(x) for x in rows]
+def eliminate(gram, n):
+    a = jnp.where(iota((n, 128), 1) == iota((n, 128), 0) + n, 1.0, gram)
+    done = []
     for k in range(n):
-        kb, ks = divmod(k, 8)
-        ga, ia = rows[kb]
-        pivot = ga[ks:ks + 1, k:k + 1]
-        inv = lax.rsqrt(pivot)
-        grow, irow = ga[ks:ks + 1, :] * inv, ia[ks:ks + 1, :] * inv
-        done[kb][ks] = (grow, irow)
-        for q in range(kb, len(rows)):
-            col = rows[q][0][:, k:k + 1] * inv
-            rows[q] = [rows[q][0] - col * grow, rows[q][1] - col * irow]
-    return done
-
-
-def factor_kernel(dims, s_hbm, res_ref, gram_ref, q_ref, r_ref, s_ref, sem):
+        if k % 8 == 0 and k > 0:
+            a = a[8:]
+        ks = k % 8
+        inv = lax.rsqrt(a[ks:ks + 1, k:k + 1])
+        row = a[ks:ks + 1, :] * inv
+        done.append(row)
+        a = a - (a[:, k:k + 1] * inv) * row
+    return jnp.concatenate(done, axis=0)
+
+
+def factor_kernel(dims, s_hbm, res_ref, gram_ref, fac_ref, q_ref, r_ref, s_ref, sem):
     M, R, C, D, J, X, I, Y, A, B, F, G = dims
     K = D + B
     cp = pltpu.make_async_copy(s_hbm, s_ref, sem)
     cp.start()
-    eye_row, eye_col = iota((8, 128), 0), iota((8, 128), 1)
-    rows = [[gram_ref[8 * q:8 * q + 8, :], jnp.where(eye_col == eye_row + 8 * q, 1.0, 0.0)] for q in range(K // 8)]
-    done = eliminate(rows, K)
-    upper = jnp.concatenate([x[0] for blk in done for x in blk], axis=0)[:, :K]
-    w = jnp.concatenate([x[1] for blk in done for x in blk], axis=0)[:, :K]
+    exact = functools.partial(lax.dot_general, precision=lax.Precision.HIGHEST, preferred_element_type=F32)
+    NN = (((1,), (0,)), ((), ()))
+    u11, w11 = fac_ref[:, :D], fac_ref[:, D:2 * D]
+    g21 = gram_ref[:, :D]
+    l21 = exact(g21, w11, NT)
+    u12 = exact(w11, g21, NT)
+    s22 = gram_ref[:, D:K] - exact(l21, l21, NT)
+    last = eliminate(jnp.concatenate([s22, jnp.zeros((B, 128 - B), F32)], axis=1), B)
+    u22, w22 = last[:, :B], last[:, B:2 * B]
+    w21 = -exact(w22, exact(l21, w11, NN), NN)
+    upper = jnp.concatenate(
+        [jnp.concatenate([u11, u12], axis=1), jnp.concatenate([jnp.zeros((B, D), F32), u22], axis=1)], axis=0)
+    w = jnp.concatenate(
+        [jnp.concatenate([w11, jnp.zeros((D, B), F32)], axis=1), jnp.concatenate([w21, w22], axis=1)], axis=0)
     tri = iota((K, K), 1) >= iota((K, K), 0)
     r_ref[...] = jnp.where(tri, upper, 0.0)
     w_hi, w_lo = split2(w)
@@ -309,11 +332,12 @@
     vmem = pl.BlockSpec(memory_space=pltpu.VMEM)
     hbm = pl.BlockSpec(memory_space=pl.ANY)
     DMA = pltpu.SemaphoreType.DMA
-    res, gram = pl.pallas_call(
+    res, gram, fac = pl.pallas_call(
         functools.partial(term_kernel, dims),
-        out_shape=(jax.ShapeDtypeStruct((C * B, I), F32), jax.ShapeDtypeStruct((K, 128), F32)),
+        out_shape=(jax.ShapeDtypeStruct((C * B, I), F32), jax.ShapeDtypeStruct((B, 128), F32),
+                   jax.ShapeDtypeStruct((D, 128), F32)),
         in_specs=[hbm] * 7,
-        out_specs=(vmem, vmem),
+        out_specs=(vmem, vmem, vmem),
         scratch_shapes=[
             pltpu.VMEM(ri.shape, BF16),
             pltpu.VMEM(rl.shape, BF16),
@@ -329,9 +353,10 @@
             pltpu.VMEM((A * B, I), F32),
             pltpu.VMEM((A * B, I), BF16),
             pltpu.VMEM((M, C * B, I), BF16),
-            pltpu.VMEM((M * R, K, 128), F32),
+            pltpu.VMEM((M * R, B, 128), F32),
+            pltpu.VMEM((M * R, D, 128), F32),
             DMA((7,)), DMA((R,)), DMA((R,)), DMA((R,)), DMA((R,)),
-            DMA((R,)), DMA((M,)), DMA((M * R,)), DMA((M * R,)),
+            DMA((R,)), DMA((M,)), DMA((M * R,)), DMA((M * R,)), DMA((M * R,)), DMA((M * R,)),
         ],
         compiler_params=pltpu.CompilerParams(
             collective_id=0, has_side_effects=True, vmem_limit_bytes=62 * 1024 * 1024),
@@ -339,11 +364,11 @@
     q, r_factor = pl.pallas_call(
         functools.partial(factor_kernel, dims),
         out_shape=(jax.ShapeDtypeStruct((C, K, I), F32), jax.ShapeDtypeStruct((K, K), F32)),
-        in_specs=[hbm, vmem, vmem],
+        in_specs=[hbm, vmem, vmem, vmem],
         out_specs=(vmem, vmem),
         scratch_shapes=[pltpu.VMEM(s.shape, BF16), DMA],
         compiler_params=pltpu.CompilerParams(vmem_limit_bytes=62 * 1024 * 1024),
-    )(s, res, gram)
+    )(s, res, gram, fac)
     return q.transpose(0, 2, 1), r_factor
 
 
@@ -392,7 +417,7 @@
     B = right_interface.shape[2]
     tiles = (
         n_mode == n_rank and J == 128 and I == 128 and rhs_core.shape[1] == I
-        and C % 16 == 0 and B == 16 and D % 16 == 0 and D + B <= 128
+        and C % 16 == 0 and B == 16 and D % 16 == 0 and D + B <= 128 and 2 * D <= 128
         and 256 % Y == 0 and (256 // Y) % 16 == 0 and X % 2 == 0
     )
     return (fused if tiles else plain)(n_mode, n_rank, *args)

time: 29.3 us -> 26.2 us (0.89)
  Pallas kernels: 28.5 us -> 25.4 us
    pallas_call x1, Pallas kernels: 9.05 us -> 4.52 us  [fused(): pl.pallas_call(functools.partial(factor_kernel, dims), out_shape=(jax.Sha...]
    pallas_call x1, Pallas kernels: 19.5 us -> 20.9 us  [fused(): pl.pallas_call(functools.partial(term_kernel, dims), out_shape=(jax.Shape...]
where the time goes in v3:
time: 26.2 us; the launch traced here: 26 us
  Pallas kernels  25.4 us (97%)
  between operations  0.64 us (2%)
    pallas_call x1, Pallas kernels, fused(): pl.pallas_call(functools.partial(term_kernel, dims), out_shape=(jax.Shape...  20.9 us
    pallas_call x1, Pallas kernels, fused(): pl.pallas_call(functools.partial(factor_kernel, dims), out_shape=(jax.Sha...  4.52 us

profile of v3, /device:TPU:0, one launch (start us, length us, event | category | flops | bytes accessed | tf_op | source)
XLA Modules:
  0.0 26.0 jit_solution(3666724780079209196)
XLA Ops:
  0.6 20.9 %shard_map.86 = (f32[512,128]{1,0:T(8,128)}, f32[16,128]{1,0:T(8,128)}, f32[64,128]{1,0:T(8,128)}) custom-call(bf16[2048,128]{1,0:T(8,128)(2,1)} %bitcast.18, bf16[8192,128]{1,0:T(8,128)(2,1)} %bitcast.17, bf16[256,64]{1,0:T(8,128)(2,1)} %bitcast.20, bf16[128,64]{1,0:T(8,128)(2,1)} %bitcast.22, bf16[16,32]{1,0:T(8,128)(2,1)} %bitcast.23, ...), custom_call_target="tpu_custom_call" | custom-call | tf_op jit(solution)/shard_map/pallas_call | solution.py:335
  21.5 4.5 %shard_map.87 = (f32[32,80,128]{2,1,0:T(8,128)}, f32[80,80]{1,0:T(8,128)}) custom-call(bf16[2048,128]{1,0:T(8,128)(2,1)} %bitcast.19, f32[512,128]{1,0:T(8,128)} %get-tuple-element.7.res_ref, f32[16,128]{1,0:T(8,128)} %get-tuple-element.8.gram_ref, f32[64,128]{1,0:T(8,128)} %get-tuple-element.9.fac_ref), custom_call_target="tpu_custom_call" | custom-call | tf_op jit(solution)/shard_map/pallas_call | solution.py:364

commit v4 on v3

--- a/solution.py
+++ b/solution.py
@@ -50,6 +50,7 @@
     m, r = lax.axis_index("mode"), lax.axis_index("rank")
     CT = C * R
     K = D + B
+    AB, FG = C * B, F * G
 
     def others(f):
         for mm_ in range(M):
@@ -77,34 +78,33 @@
         cp.start()
     cp_s.wait()
     cp_l.wait()
-    pl.semaphore_wait(barrier, M * R - 1)
-
-    def s_copy(rr_):
-        return pltpu.make_async_remote_copy(
-            src_ref=s_all.at[r], dst_ref=s_all.at[r], send_sem=s_send.at[rr_], recv_sem=s_recv.at[r],
-            device_id={"rank": rr_}, device_id_type=MESH)
-
-    def l_copy(rr_):
-        return pltpu.make_async_remote_copy(
-            src_ref=l_all.at[r], dst_ref=l_all.at[r], send_sem=l_send.at[rr_], recv_sem=l_recv.at[r],
-            device_id={"rank": rr_}, device_id_type=MESH)
-
-    def over_rank(f):
-        for rr_ in range(R):
-            pl.when(rr_ != r)(functools.partial(f, rr_))
-
-    def start_sl(rr_):
-        s_copy(rr_).start()
-        l_copy(rr_).start()
-
-    over_rank(start_sl)
-
     me = m * R + r
     gs = jnp.zeros((D, D), F32)
     for a2 in range(C // 2):
         e = jnp.concatenate([s_all[r, a * D:(a + 1) * D, :] for a in (2 * a2, 2 * a2 + 1)], axis=1)
         gs = gs + mm_nt(e, e)
     gs_all[me] = jnp.concatenate([gs, jnp.zeros((D, 128 - D), F32)], axis=1)
+    pl.semaphore_wait(barrier, M * R - 1)
+
+    def s_copy(rr_):
+        return pltpu.make_async_remote_copy(
+            src_ref=s_all.at[r], dst_ref=s_all.at[r], send_sem=s_send.at[rr_], recv_sem=s_recv.at[r],
+            device_id={"rank": rr_}, device_id_type=MESH)
+
+    def l_copy(rr_):
+        return pltpu.make_async_remote_copy(
+            src_ref=l_all.at[r], dst_ref=l_all.at[r], send_sem=l_send.at[rr_], recv_sem=l_recv.at[r],
+            device_id={"rank": rr_}, device_id_type=MESH)
+
+    def over_rank(f):
+        for rr_ in range(R):
+            pl.when(rr_ != r)(functools.partial(f, rr_))
+
+    def start_sl(rr_):
+        s_copy(rr_).start()
+        l_copy(rr_).start()
+
+    over_rank(start_sl)
 
     def sums(buf, send, recv):
         def copy(who, mm_, rr_):
@@ -152,18 +152,6 @@
 
     for cp in small:
         cp.wait()
-
-    AB, FG = C * B, F * G
-    row_ab, col_fg = iota((AB, 1), 0), iota((1, FG), 1)
-    pick_a = one_hot(row_ab // B == iota((AB, C), 1))
-    pick_b = one_hot(row_ab % B == iota((AB, B), 1))
-    pick_f = one_hot(iota((F, FG), 0) == col_fg // G)
-    pick_g = one_hot(iota((G, FG), 0) == col_fg % G)
-    left = mm(mm_nt(pick_a, rl_ref[...]).astype(BF16), pick_f)
-    right = mm(mm_nt(pick_b, rr_ref[...]).astype(BF16), pick_g)
-    k_hi, k_lo = split2(left * right)
-    rc = rc_ref[...]
-    res_ref[...] = mm(k_hi, rc) + mm(k_lo, rc)
 
     ri_t = ri_ref[...]
     perm_cb = turn(16 * B, B, 16)
@@ -206,7 +194,7 @@
         a_ref[x2] = mm_nt(z_ref[...], w).astype(BF16)
         return carry
 
-    lax.fori_loop(0, X // 2, main_step, 0)
+    lax.fori_loop(0, X // 2, main_step, 0, unroll=True)
 
     l2 = jnp.concatenate([l_all[rr_] for rr_ in range(R)], axis=0).astype(F32).T.astype(BF16)
     for b2 in range(B // 2):
@@ -233,6 +221,17 @@
         pl.when(jnp.logical_not(local & (rr_ == r)))(lambda rr_=rr_: t_copy(rr_).start())
 
     fac_ref[...] = eliminate(gs_finish(), D)
+
+    row_ab, col_fg = iota((AB, 1), 0), iota((1, FG), 1)
+    pick_a = one_hot(row_ab // B == iota((AB, C), 1))
+    pick_b = one_hot(row_ab % B == iota((AB, B), 1))
+    pick_f = one_hot(iota((F, FG), 0) == col_fg // G)
+    pick_g = one_hot(iota((G, FG), 0) == col_fg % G)
+    left = mm(mm_nt(pick_a, rl_ref[...]).astype(BF16), pick_f)
+    right = mm(mm_nt(pick_b, rr_ref[...]).astype(BF16), pick_g)
+    k_hi, k_lo = split2(left * right)
+    rc = rc_ref[...]
+    res_ref[...] = mm(k_hi, rc) + mm(k_lo, rc)
 
     @pl.when(local)
     def _():
@@ -279,7 +278,7 @@
     return jnp.concatenate(done, axis=0)
 
 
-def factor_kernel(dims, s_hbm, res_ref, gram_ref, fac_ref, q_ref, r_ref, s_ref, sem):
+def factor_kernel(dims, s_hbm, res_ref, gram_ref, fac_ref, q_hbm, r_ref, s_ref, q_ref, sem, q_sem):
     M, R, C, D, J, X, I, Y, A, B, F, G = dims
     K = D + B
     cp = pltpu.make_async_copy(s_hbm, s_ref, sem)
@@ -304,6 +303,7 @@
     lhs = jnp.concatenate([w_hi, w_hi[:, D:], w_lo], axis=1)
     hi, lo = split2(res_ref[...])
     cp.wait()
+    outs = []
     for a2 in range(C // 2):
         cols = []
         for a in (2 * a2, 2 * a2 + 1):
@@ -312,6 +312,13 @@
         q = mm(lhs, jnp.concatenate(cols, axis=1))
         q_ref[2 * a2] = q[:, :I]
         q_ref[2 * a2 + 1] = q[:, I:]
+        if (2 * a2 + 2) % 8 == 0:
+            part = pl.ds(2 * a2 - 6, 8)
+            out = pltpu.make_async_copy(q_ref.at[part], q_hbm.at[part], q_sem.at[a2 // 4])
+            out.start()
+            outs.append(out)
+    for out in outs:
+        out.wait()
 
 
 def fused(n_mode, n_rank, solution_core, operator_core, left_interface, right_interface, rhs_left, rhs_core, rhs_right):
@@ -365,8 +372,8 @@
         functools.partial(factor_kernel, dims),
         out_shape=(jax.ShapeDtypeStruct((C, K, I), F32), jax.ShapeDtypeStruct((K, K), F32)),
         in_specs=[hbm, vmem, vmem, vmem],
-        out_specs=(vmem, vmem),
-        scratch_shapes=[pltpu.VMEM(s.shape, BF16), DMA],
+        out_specs=(hbm, vmem),
+        scratch_shapes=[pltpu.VMEM(s.shape, BF16), pltpu.VMEM((C, K, I), F32), DMA, DMA((C // 8,))],
         compiler_params=pltpu.CompilerParams(vmem_limit_bytes=62 * 1024 * 1024),
     )(s, res, gram, fac)
     return q.transpose(0, 2, 1), r_factor

time: 26.2 us -> 25.2 us (0.962)
  Pallas kernels: 25.4 us -> 24.4 us
    pallas_call x1, Pallas kernels: 20.9 us -> 19.4 us  [fused(): pl.pallas_call(functools.partial(term_kernel, dims), out_shape=(jax.Shape...]
    pallas_call x1, Pallas kernels: 4.52 us -> 5.02 us  [fused(): pl.pallas_call(functools.partial(factor_kernel, dims), out_shape=(jax.Sha...]
where the time goes in v4:
time: 25.2 us; the launch traced here: 25.1 us
  Pallas kernels  24.4 us (97%)
  between operations  0.64 us (3%)
    pallas_call x1, Pallas kernels, fused(): pl.pallas_call(functools.partial(term_kernel, dims), out_shape=(jax.Shape...  19.4 us
    pallas_call x1, Pallas kernels, fused(): pl.pallas_call(functools.partial(factor_kernel, dims), out_shape=(jax.Sha...  5.02 us

profile of v4, /device:TPU:0, one launch (start us, length us, event | category | flops | bytes accessed | tf_op | source)
XLA Modules:
  0.0 25.1 jit_solution(18391584388714939144)
XLA Ops:
  0.6 19.4 %shard_map.86 = (f32[512,128]{1,0:T(8,128)}, f32[16,128]{1,0:T(8,128)}, f32[64,128]{1,0:T(8,128)}) custom-call(bf16[2048,128]{1,0:T(8,128)(2,1)} %bitcast.18, bf16[8192,128]{1,0:T(8,128)(2,1)} %bitcast.17, bf16[256,64]{1,0:T(8,128)(2,1)} %bitcast.20, bf16[128,64]{1,0:T(8,128)(2,1)} %bitcast.22, bf16[16,32]{1,0:T(8,128)(2,1)} %bitcast.23, ...), custom_call_target="tpu_custom_call" | custom-call | tf_op jit(solution)/shard_map/pallas_call | solution.py:342
  20.0 5.0 %shard_map.87 = (f32[32,80,128]{2,1,0:T(8,128)}, f32[80,80]{1,0:T(8,128)}) custom-call(bf16[2048,128]{1,0:T(8,128)(2,1)} %bitcast.19, f32[512,128]{1,0:T(8,128)} %get-tuple-element.7.res_ref, f32[16,128]{1,0:T(8,128)} %get-tuple-element.8.gram_ref, f32[64,128]{1,0:T(8,128)} %get-tuple-element.9.fac_ref), custom_call_target="tpu_custom_call" | custom-call | tf_op jit(solution)/shard_map/pallas_call | solution.py:371

commit v5 on v4

--- a/solution.py
+++ b/solution.py
@@ -148,7 +148,7 @@
                     out[y * per:(y + 1) * per, h * J:(h + 1) * J])
         return carry
 
-    lax.fori_loop(0, X * I * Y // 512, op_step, 0, unroll=4)
+    lax.fori_loop(0, X * I * Y // 512, op_step, 0, unroll=True)
 
     for cp in small:
         cp.wait()

time: 25.2 us -> 24.7 us (0.980)
  Pallas kernels: 24.4 us -> 23.9 us
    pallas_call x1, Pallas kernels: 19.4 us -> 18.8 us  [fused(): pl.pallas_call(functools.partial(term_kernel, dims), out_shape=(jax.Shape...]
where the time goes in v5:
time: 24.7 us; the launch traced here: 24.5 us
  Pallas kernels  23.9 us (97%)
  between operations  0.64 us (3%)
    pallas_call x1, Pallas kernels, fused(): pl.pallas_call(functools.partial(term_kernel, dims), out_shape=(jax.Shape...  18.8 us
    pallas_call x1, Pallas kernels, fused(): pl.pallas_call(functools.partial(factor_kernel, dims), out_shape=(jax.Sha...  5.02 us

profile of v5, /device:TPU:0, one launch (start us, length us, event | category | flops | bytes accessed | tf_op | source)
XLA Modules:
  0.0 24.5 jit_solution(13032285937147420037)
XLA Ops:
  0.6 18.8 %shard_map.86 = (f32[512,128]{1,0:T(8,128)}, f32[16,128]{1,0:T(8,128)}, f32[64,128]{1,0:T(8,128)}) custom-call(bf16[2048,128]{1,0:T(8,128)(2,1)} %bitcast.18, bf16[8192,128]{1,0:T(8,128)(2,1)} %bitcast.17, bf16[256,64]{1,0:T(8,128)(2,1)} %bitcast.20, bf16[128,64]{1,0:T(8,128)(2,1)} %bitcast.22, bf16[16,32]{1,0:T(8,128)(2,1)} %bitcast.23, ...), custom_call_target="tpu_custom_call" | custom-call | tf_op jit(solution)/shard_map/pallas_call | solution.py:342
  19.5 5.0 %shard_map.87 = (f32[32,80,128]{2,1,0:T(8,128)}, f32[80,80]{1,0:T(8,128)}) custom-call(bf16[2048,128]{1,0:T(8,128)(2,1)} %bitcast.19, f32[512,128]{1,0:T(8,128)} %get-tuple-element.7.res_ref, f32[16,128]{1,0:T(8,128)} %get-tuple-element.8.gram_ref, f32[64,128]{1,0:T(8,128)} %get-tuple-element.9.fac_ref), custom_call_target="tpu_custom_call" | custom-call | tf_op jit(solution)/shard_map/pallas_call | solution.py:371
